TPU v7x, 128 devices: a whole 4x4x4 slice. The times are simulated.
128 devices in a mesh: arc: 8 (over y, x_hi), trow: 4 (over z), tcol: 4 (over x_lo, core).
Axes of the slice: x: 4 (x_hi: 2, x_lo: 2; x = x_hi * 2 + x_lo), y: 4, z: 4, core: 2. Of those that a mesh axis runs over, the one named last changes fastest.
Arguments:
- design: bfloat16 [5120, 8192], P('arc', 'tcol'), may hold values from -0.125 to 0.125
- local_design: bfloat16 [5120, 128], P('arc'), may hold values from -0.3125 to 0.3125
- lengths: int32 [16], P('arc'), may hold values from 1 to 320, 3840 in all
- regularizer: float32 [8192], P(('arc', 'trow')), may hold values from 0.2 to 2
Outputs:
- normal: float32 [8192, 8192], P(('arc', 'trow'), 'tcol')
- panel_factor: float32 [2, 8192, 512], P(None, 'tcol')
Inputs may be any that keep to these rules, and one draw needn't show every extreme that they name: `lengths`: each arc has at least one live row; some arc is full.
All inputs are finite; a program needn't handle non-finite values. No bound on the sum of `lengths` on one device may be relied on, other than what follows from the above.
Results may differ from a plain program's by a relative error of at most 0.003.
Values may be sent and summed in bfloat16 or wider, within the bound.
A program may use at most 128 MiB of HBM per device.

v0:
```python
import jax
import jax.numpy as jnp
from jax import lax
from jax.sharding import PartitionSpec as P

PANEL = 512
PANELS = 2
ridge = 0.1


def broadcast(block, axis, holder):
    block = jnp.where(lax.axis_index(axis) == holder, block, jnp.zeros_like(block))
    return lax.psum(block, axis)


def project_arcs(design, local_design, lengths):
    arc_count = lengths.shape[0]
    row_count = design.shape[0]
    capacity = row_count // arc_count
    arc_blocks = design.reshape(arc_count, capacity, design.shape[1])
    local_half = local_design.reshape(arc_count, capacity, local_design.shape[1])
    live_rows = jnp.arange(capacity, dtype=jnp.int32)[None, :] < lengths[:, None]
    arc_blocks = jnp.where(live_rows[:, :, None], arc_blocks, jnp.zeros((), design.dtype))
    local_half = jnp.where(live_rows[:, :, None], local_half, jnp.zeros((), local_design.dtype))
    local_normal = jnp.einsum(
        "acl,acm->alm", local_half, local_half, preferred_element_type=jnp.float32
    )
    local_normal = local_normal + ridge * jnp.eye(local_half.shape[2], dtype=jnp.float32)[None]
    local_factor = jnp.linalg.cholesky(local_normal)
    local_cols = local_half.astype(jnp.float32)
    basis_rows = lax.linalg.triangular_solve(
        local_factor, jnp.transpose(local_cols, (0, 2, 1)), left_side=True, lower=True
    )
    basis_rows = basis_rows.astype(jnp.bfloat16)
    loadings = jnp.einsum(
        "alc,acw->alw", basis_rows, arc_blocks, preferred_element_type=jnp.float32
    ).astype(jnp.bfloat16)
    cleaned = arc_blocks.astype(jnp.float32) - jnp.einsum(
        "alc,alw->acw", basis_rows, loadings, preferred_element_type=jnp.float32
    )
    return cleaned.astype(jnp.bfloat16).reshape(row_count, design.shape[1])


def contract_rows(left_rows, right_rows):
    return lax.dot_general(
        left_rows, right_rows, (((0,), (0,)), ((), ())), preferred_element_type=jnp.float32
    )


def per_device(design, local_design, lengths, regularizer):
    row_count, col_width = design.shape
    tile_rows = regularizer.shape[0]
    arc_total = lax.axis_size("arc")
    trow_total = lax.axis_size("trow")
    trow_index = lax.axis_index("trow")
    row_start = (lax.axis_index("arc") * trow_total + trow_index) * tile_rows
    col_start = lax.axis_index("tcol") * col_width
    projected = project_arcs(design, local_design, lengths)
    gathered = lax.all_gather(projected, "tcol", axis=1, tiled=True)
    regrouped = gathered.reshape(row_count, arc_total, trow_total, tile_rows)
    selected = lax.dynamic_slice_in_dim(regrouped, trow_index, 1, 2).reshape(
        row_count, arc_total * tile_rows
    )
    normal_block = lax.psum_scatter(
        contract_rows(selected, projected), "arc", scatter_dimension=0, tiled=True
    )
    rows_global = row_start + jnp.arange(tile_rows, dtype=jnp.int32)
    cols_global = col_start + jnp.arange(col_width, dtype=jnp.int32)
    on_diagonal = rows_global[:, None] == cols_global[None, :]
    normal_block = normal_block + jnp.where(
        on_diagonal, regularizer[:, None], jnp.zeros((), jnp.float32)
    )
    panel_factors = []
    for panel_index in range(PANELS):
        lead_col = panel_index * PANEL
        padded_rows = jnp.pad(normal_block, ((PANEL, PANEL), (0, 0)))
        slice_start = jnp.clip(lead_col - row_start + PANEL, 0, tile_rows + PANEL)
        slice_rows = lax.dynamic_slice_in_dim(padded_rows, slice_start, PANEL, 0)
        panel_global = lead_col + jnp.arange(PANEL, dtype=jnp.int32)
        in_tile = (panel_global >= row_start) & (panel_global < row_start + tile_rows)
        own_share = jnp.where(in_tile[:, None], slice_rows, jnp.zeros((), jnp.float32))
        panel_strip = lax.psum(own_share, ("arc", "trow"))
        pivot_block, row_strip = (
            broadcast(panel_strip[:, lead_col : lead_col + PANEL], "tcol", 0),
            broadcast(normal_block[:, lead_col : lead_col + PANEL], "tcol", 0),
        )
        lower_factor = jnp.linalg.cholesky(pivot_block)
        col_factor = lax.linalg.triangular_solve(
            lower_factor, panel_strip, left_side=True, lower=True
        ).T
        row_factor = lax.linalg.triangular_solve(
            lower_factor, row_strip.T, left_side=True, lower=True
        ).T
        col_factor = jnp.where(
            cols_global[:, None] >= lead_col, col_factor, jnp.zeros((), jnp.float32)
        )
        row_factor = jnp.where(
            rows_global[:, None] >= lead_col, row_factor, jnp.zeros((), jnp.float32)
        )
        normal_block = normal_block - jnp.dot(
            row_factor, col_factor.T, precision=lax.Precision.HIGHEST
        )
        panel_factors.append(col_factor)
    return (normal_block, jnp.stack(panel_factors))


def solution(mesh):
    return jax.shard_map(
        per_device,
        mesh=mesh,
        in_specs=(P("arc", "tcol"), P("arc", None), P("arc"), P(("arc", "trow"))),
        out_specs=(P(("arc", "trow"), "tcol"), P(None, "tcol", None)),
        check_vma=False,
    )
```

profile of v0, /device:TPU:1, one launch (start us, length us, event | category | flops | bytes accessed | tf_op | source)
XLA Modules:
  0.0 1569.1 jit_solution(3386765637183662593)
XLA Ops:
  9.6 23.5 %custom-call.33 = f32[2,128,128]{2,1,0:T(8,128)S(1)} custom-call(f32[2,128,128]{2,1,0:T(8,128)S(1)} %fusion.97), custom_call_target="Cholesky" | custom-call | tf_op jit(solution)/shard_map/jit(cholesky)/cholesky | solution.py:29
  33.4 19.7 %custom-call.34 = f32[2,1,128,128]{2,3,1,0:T(8,128)S(1)} custom-call(f32[2,1,128,128]{3,2,1,0:T(8,128)S(1)} %select_bitcast_fusion), custom_call_target="InvertDiagBlocksLowerTriangular" | custom-call | tf_op jit(solution)/shard_map/triangular_solve | solution.py:31
  61.2 102.4 %all-gather.2.cloned.1.call-done = bf16[640,8192]{0,1:T(8,128)(2,1)} async-done(((bf16[640,2048]{0,1:T(8,128)(2,1)}), bf16[640,8192]{0,1:T(8,128)(2,1)}) %all-gather.2.cloned.1.call-update) | async-done | bytes 10485776 | tf_op jit(solution)/shard_map/all_gather | solution.py:59
  165.6 10.2 fusion.158
  175.9 190.4 %reduce-scatter.2.cloned.1.call-done = f32[256,2048]{0,1:T(8,128)} async-done(((f32[2048,2048]{0,1:T(8,128)}), f32[256,2048]{0,1:T(8,128)}) %reduce-scatter.2.cloned.1.call-update) | async-done | bytes 2097168 | tf_op jit(solution)/shard_map/reduce_scatter | solution.py:64
  372.1 345.6 %all-reduce.10.cloned.1.call-done = f32[512,2048]{0,1:T(8,128)} async-done(((f32[512,2048]{0,1:T(8,128)}), f32[512,2048]{0,1:T(8,128)}) %all-reduce.10.cloned.1.call-update) | async-done | bytes 4194320 | tf_op jit(solution)/shard_map/psum | solution.py:82
  720.2 71.5 %all-reduce.16.cloned.1.call-done = (f32[512,512]{0,1:T(8,128)}, f32[512,256]{1,0:T(8,128)}) async-done(((f32[512,512]{0,1:T(8,128)}, f32[512,256]{1,0:T(8,128)}), (f32[512,512]{0,1:T(8,128)}, f32[512,256]{1,0:T(8,128)})) %all-reduce.16.cloned.1.call-update) | async-done | bytes 1572880 | tf_op jit(solution)/shard_map/psum | solution.py:13
  794.7 11.7 cholesky.327
  806.6 9.8 custom-call.40
  817.1 11.7 cholesky.346
  828.8 10.2 custom-call.41
  839.7 11.7 cholesky.367
  851.5 9.8 custom-call.42
  861.9 11.7 cholesky.384
  878.9 7.7 while.8
  886.6 39.3 %custom-call.43 = f32[4,128,128]{1,2,0:T(8,128)S(1)} custom-call(f32[4,128,128]{2,1,0:T(8,128)S(1)} %get-tuple-element.33), custom_call_target="InvertDiagBlocksLowerTriangular" | custom-call | tf_op jit(solution)/shard_map/triangular_solve/custom-call.9 | solution.py:91
  935.1 4.7 convolution_subtract_fusion.3
  942.2 7.2 fusion.17
  966.0 342.8 %all-reduce.12.cloned.1.call-done = f32[512,2048]{0,1:T(8,128)} async-done(((f32[512,2048]{0,1:T(8,128)}), f32[512,2048]{0,1:T(8,128)}) %all-reduce.12.cloned.1.call-update) | async-done | bytes 4194320 | tf_op jit(solution)/shard_map/psum | solution.py:82
  1314.6 68.2 %all-reduce.14.cloned.1.call-done = (f32[512,512]{0,1:T(8,128)}, f32[512,256]{1,0:T(8,128)}) async-done(((f32[512,512]{0,1:T(8,128)}, f32[512,256]{1,0:T(8,128)}), (f32[512,512]{0,1:T(8,128)}, f32[512,256]{1,0:T(8,128)})) %all-reduce.14.cloned.1.call-update) | async-done | bytes 1572880 | tf_op jit(solution)/shard_map/psum | solution.py:13
  1385.7 11.7 cholesky.399
  1397.6 9.8 custom-call.45
  1408.1 11.7 cholesky.418
  1419.8 10.2 custom-call.46
  1430.7 11.7 cholesky.439
  1442.5 9.8 custom-call.47
  1452.9 11.7 cholesky.456
  1469.9 7.7 while.9
  1477.6 39.3 %custom-call.48 = f32[4,128,128]{1,2,0:T(8,128)S(1)} custom-call(f32[4,128,128]{2,1,0:T(8,128)S(1)} %get-tuple-element.35), custom_call_target="InvertDiagBlocksLowerTriangular" | custom-call | tf_op jit(solution)/shard_map/triangular_solve/custom-call.9 | solution.py:91
  1526.0 4.7 convolution_subtract_fusion.2
  1533.2 7.1 fusion.14
  1554.2 7.8 pad_maximum_fusion
  (184 shorter events, 111.2 us)
Async XLA Ops:
  7.2 156.4 %all-gather.2.cloned.1.call-start = ((), (), s32[]{:S(2)}) async-start(), calls=%async_computation.1 | async-start | bytes 13107200 | tf_op jit(solution)/shard_map/all_gather | solution.py:59
  61.0 305.3 %reduce-scatter.2.cloned.1.call-start = ((), (), s32[]{:S(2)}) async-start(), calls=%async_computation.2 | async-start | bytes 18874368 | tf_op jit(solution)/shard_map/reduce_scatter | solution.py:64
  175.8 190.5 %copy-start.18 = (f32[256]{0:T(256)S(1)}, f32[256]{0:T(256)}, u32[]{:S(2)}) copy-start(f32[256]{0:T(256)} %param.12) | copy-start | bytes 3076
  175.8 542.0 %all-reduce.10.cloned.1.call-start = ((), (), s32[]{:S(2)}) async-start(), calls=%async_computation.3 | async-start | bytes 8388608 | tf_op jit(solution)/shard_map/psum | solution.py:82
  368.0 3.3 copy-start
  371.2 420.5 %all-reduce.16.cloned.1.call-start = ((), (), s32[]{:S(2)}) async-start(), calls=%async_computation.6 | async-start | bytes 3145728 | tf_op jit(solution)/shard_map/psum | solution.py:13
  720.1 588.7 %all-reduce.12.cloned.1.call-start = ((), (), s32[]{:S(2)}) async-start(), calls=%async_computation.4 | async-start | bytes 8388608 | tf_op jit(solution)/shard_map/psum | solution.py:82
  886.6 48.4 %copy-start.3 = (f32[512,512]{1,0:T(8,128)}, f32[512,512]{1,0:T(8,128)S(1)}, u32[]{:S(2)}) copy-start(f32[512,512]{1,0:T(8,128)S(1)} %get-tuple-element.206) | copy-start | bytes 3145732
  942.2 8.3 copy-start.16
  942.2 13.2 copy-start.1
  942.2 13.2 copy-start.4
  942.2 13.2 copy-start.6
  942.2 13.2 copy-start.8
  950.5 8.9 copy-start.10
  959.4 1.3 copy-start.14
  963.9 347.3 %copy-start.5 = (f32[128,2048]{0,1:T(8,128)S(1)}, f32[128,2048]{0,1:T(8,128)}, u32[]{:S(2)}) copy-start(f32[128,2048]{0,1:T(8,128)} %copy.69) | copy-start | bytes 3145732
  963.9 347.3 %copy-start.7 = (f32[128,2048]{0,1:T(8,128)S(1)}, f32[128,2048]{0,1:T(8,128)}, u32[]{:S(2)}) copy-start(f32[128,2048]{0,1:T(8,128)} %copy.70) | copy-start | bytes 3145732
  963.9 347.3 %copy-start.9 = (f32[128,2048]{0,1:T(8,128)S(1)}, f32[128,2048]{0,1:T(8,128)}, u32[]{:S(2)}) copy-start(f32[128,2048]{0,1:T(8,128)} %copy.71) | copy-start | bytes 3145732
  963.9 418.8 %all-reduce.14.cloned.1.call-start = ((), (), s32[]{:S(2)}) async-start(), calls=%async_computation.5 | async-start | bytes 3145728 | tf_op jit(solution)/shard_map/psum | solution.py:13
  1477.6 48.4 %copy-start.2 = (f32[512,512]{1,0:T(8,128)}, f32[512,512]{1,0:T(8,128)S(1)}, u32[]{:S(2)}) copy-start(f32[512,512]{1,0:T(8,128)S(1)} %get-tuple-element.205) | copy-start | bytes 3145732
  1533.2 8.1 copy-start.17
  1533.2 13.0 copy-start.11
  1533.2 13.0 copy-start.12
  1533.2 13.0 copy-start.13
  1546.2 2.5 copy-start.15
Sparse Core Ops, SparseCore 0:
  61.1 102.4 all-gather.1
  175.9 190.3 reduce-scatter.1
  371.4 346.3 all-reduce.9
  721.0 70.6 all-reduce.15
  964.0 344.7 all-reduce.11
  1312.0 70.6 all-reduce.13
where the time goes:
time: 1580 us; the launch traced here: 1570 us
  waiting for transfers between devices  1120 us (71%)
  other arithmetic  314 us (20%)
  matrix products  78.7 us (5%)
  local copies, waits for them, and re-layouts  34.9 us (2%)
  between operations  20 us (1%)
    psum x2, waiting for transfers between devices, per_device(): panel_strip = lax.psum(own_share, ('arc', 'trow'))  688 us
    reduce_scatter x1, waiting for transfers between devices, per_device(): lax.psum_scatter(contract_rows(selected, projected), 'arc', scatter_dimen...  190 us
    another operation x30, other arithmetic, per_device(): lower_factor = jnp.linalg.cholesky(pivot_block)  159 us
    psum x2, waiting for transfers between devices, broadcast(): return lax.psum(block, axis)  140 us
    all_gather x1, waiting for transfers between devices, per_device(): gathered = lax.all_gather(projected, 'tcol', axis=1, tiled=True)  102 us
    another operation x5, other arithmetic, per_device(): lax.linalg.triangular_solve(lower_factor, row_strip.T, left_side=True, lo...  79.2 us
    another operation x14, matrix products, per_device(): lax.linalg.triangular_solve(lower_factor, panel_strip, left_side=True, lo...  40.7 us
  transfers between devices with their start and end apart: 6, of which 6 were waited for; matrix products, arithmetic and copies ran while one was open for 0% of the time, Pallas kernels for 0%

commit v1 on v0

--- a/solution.py
+++ b/solution.py
@@ -79,7 +79,9 @@
         panel_global = lead_col + jnp.arange(PANEL, dtype=jnp.int32)
         in_tile = (panel_global >= row_start) & (panel_global < row_start + tile_rows)
         own_share = jnp.where(in_tile[:, None], slice_rows, jnp.zeros((), jnp.float32))
-        panel_strip = lax.psum(own_share, ("arc", "trow"))
+        panel_strip = own_share
+        for name in ("trow", "arc"):
+            panel_strip = lax.psum(panel_strip, name)
         pivot_block, row_strip = (
             broadcast(panel_strip[:, lead_col : lead_col + PANEL], "tcol", 0),
             broadcast(normal_block[:, lead_col : lead_col + PANEL], "tcol", 0),

time: 1580 us -> 1410 us (0.89)
  waiting for transfers between devices: 1120 us -> 948 us
    psum x2 -> x4, waiting for transfers between devices: 688 us -> 560 us  [per_device(): panel_strip = lax.psum(panel_strip, name)]
    psum x2, waiting for transfers between devices: 140 us -> 95.3 us  [broadcast(): return lax.psum(block, axis)]
  transfers between devices with their start and end apart: 6 -> 8, of which waited for: 6 -> 8; matrix products, arithmetic and copies ran while one was open for 0% -> 0% of each run, Pallas kernels for 0% -> 0%
where the time goes in v1:
time: 1410 us; the launch traced here: 1400 us
  waiting for transfers between devices  948 us (67%)
  other arithmetic  314 us (22%)
  matrix products  78.7 us (6%)
  local copies, waits for them, and re-layouts  35.5 us (3%)
  between operations  20.3 us (1%)
    psum x4, waiting for transfers between devices, per_device(): panel_strip = lax.psum(panel_strip, name)  560 us
    reduce_scatter x1, waiting for transfers between devices, per_device(): lax.psum_scatter(contract_rows(selected, projected), 'arc', scatter_dimen...  190 us
    another operation x30, other arithmetic, per_device(): lower_factor = jnp.linalg.cholesky(pivot_block)  159 us
    all_gather x1, waiting for transfers between devices, per_device(): gathered = lax.all_gather(projected, 'tcol', axis=1, tiled=True)  102 us
    psum x2, waiting for transfers between devices, broadcast(): return lax.psum(block, axis)  95.3 us
    another operation x5, other arithmetic, per_device(): lax.linalg.triangular_solve(lower_factor, row_strip.T, left_side=True, lo...  79.2 us
    another operation x14, matrix products, per_device(): lax.linalg.triangular_solve(lower_factor, panel_strip, left_side=True, lo...  40.7 us
  transfers between devices with their start and end apart: 8, of which 8 were waited for; matrix products, arithmetic and copies ran while one was open for 0% of the time, Pallas kernels for 0%

profile of v1, /device:TPU:1, one launch (start us, length us, event | category | flops | bytes accessed | tf_op | source)
XLA Modules:
  0.0 1397.9 jit_solution(8521776717643603738)
XLA Ops:
  9.6 23.5 %custom-call.33 = f32[2,128,128]{2,1,0:T(8,128)S(1)} custom-call(f32[2,128,128]{2,1,0:T(8,128)S(1)} %fusion.97), custom_call_target="Cholesky" | custom-call | tf_op jit(solution)/shard_map/jit(cholesky)/cholesky | solution.py:29
  33.4 19.7 %custom-call.34 = f32[2,1,128,128]{2,3,1,0:T(8,128)S(1)} custom-call(f32[2,1,128,128]{3,2,1,0:T(8,128)S(1)} %select_bitcast_fusion), custom_call_target="InvertDiagBlocksLowerTriangular" | custom-call | tf_op jit(solution)/shard_map/triangular_solve | solution.py:31
  61.2 102.4 %all-gather.2.cloned.1.call-done = bf16[640,8192]{0,1:T(8,128)(2,1)} async-done(((bf16[640,2048]{0,1:T(8,128)(2,1)}), bf16[640,8192]{0,1:T(8,128)(2,1)}) %all-gather.2.cloned.1.call-update) | async-done | bytes 10485776 | tf_op jit(solution)/shard_map/all_gather | solution.py:59
  165.6 10.2 fusion.158
  175.9 190.4 %reduce-scatter.2.cloned.1.call-done = f32[256,2048]{0,1:T(8,128)} async-done(((f32[2048,2048]{0,1:T(8,128)}), f32[256,2048]{0,1:T(8,128)}) %reduce-scatter.2.cloned.1.call-update) | async-done | bytes 2097168 | tf_op jit(solution)/shard_map/reduce_scatter | solution.py:64
  371.3 95.6 %all-reduce.12.cloned.1.call-done = f32[512,2048]{0,1:T(8,128)} async-done(((f32[512,2048]{0,1:T(8,128)}), f32[512,2048]{0,1:T(8,128)}) %all-reduce.12.cloned.1.call-update) | async-done | bytes 4194320 | tf_op jit(solution)/shard_map/psum | solution.py:84
  467.9 185.8 %all-reduce.14.cloned.1.call-done = f32[512,2048]{0,1:T(8,128)} async-done(((f32[512,2048]{0,1:T(8,128)}), f32[512,2048]{0,1:T(8,128)}) %all-reduce.14.cloned.1.call-update) | async-done | bytes 4194320 | tf_op jit(solution)/shard_map/psum | solution.py:84
  656.3 49.1 %all-reduce.22.cloned.1.call-done = (f32[512,512]{0,1:T(8,128)}, f32[512,256]{1,0:T(8,128)}) async-done(((f32[512,512]{0,1:T(8,128)}, f32[512,256]{1,0:T(8,128)}), (f32[512,512]{0,1:T(8,128)}, f32[512,256]{1,0:T(8,128)})) %all-reduce.22.cloned.1.call-update) | async-done | bytes 1572880 | tf_op jit(solution)/shard_map/psum | solution.py:13
  708.3 11.7 cholesky.327
  720.2 9.8 custom-call.40
  730.7 11.7 cholesky.346
  742.4 10.2 custom-call.41
  753.4 11.7 cholesky.367
  765.1 9.8 custom-call.42
  775.5 11.7 cholesky.384
  792.8 7.9 while.8
  800.8 39.3 %custom-call.43 = f32[4,128,128]{1,2,0:T(8,128)S(1)} custom-call(f32[4,128,128]{2,1,0:T(8,128)S(1)} %get-tuple-element.33), custom_call_target="InvertDiagBlocksLowerTriangular" | custom-call | tf_op jit(solution)/shard_map/triangular_solve/custom-call.9 | solution.py:93
  856.4 7.2 fusion.17
  878.1 93.8 %all-reduce.16.cloned.1.call-done = f32[512,2048]{0,1:T(8,128)} async-done(((f32[512,2048]{0,1:T(8,128)}), f32[512,2048]{0,1:T(8,128)}) %all-reduce.16.cloned.1.call-update) | async-done | bytes 4194320 | tf_op jit(solution)/shard_map/psum | solution.py:84
  974.0 184.9 %all-reduce.18.cloned.1.call-done = f32[512,2048]{0,1:T(8,128)} async-done(((f32[512,2048]{0,1:T(8,128)}), f32[512,2048]{0,1:T(8,128)}) %all-reduce.18.cloned.1.call-update) | async-done | bytes 4194320 | tf_op jit(solution)/shard_map/psum | solution.py:84
  1164.7 46.3 %all-reduce.20.cloned.1.call-done = (f32[512,512]{0,1:T(8,128)}, f32[512,256]{1,0:T(8,128)}) async-done(((f32[512,512]{0,1:T(8,128)}, f32[512,256]{1,0:T(8,128)}), (f32[512,512]{0,1:T(8,128)}, f32[512,256]{1,0:T(8,128)})) %all-reduce.20.cloned.1.call-update) | async-done | bytes 1572880 | tf_op jit(solution)/shard_map/psum | solution.py:13
  1214.0 11.7 cholesky.399
  1225.9 9.8 custom-call.45
  1236.3 11.7 cholesky.418
  1248.1 10.2 custom-call.46
  1259.0 11.7 cholesky.439
  1270.7 9.8 custom-call.47
  1281.1 11.7 cholesky.456
  1298.3 8.0 while.9
  1306.4 39.3 %custom-call.48 = f32[4,128,128]{1,2,0:T(8,128)S(1)} custom-call(f32[4,128,128]{2,1,0:T(8,128)S(1)} %get-tuple-element.35), custom_call_target="InvertDiagBlocksLowerTriangular" | custom-call | tf_op jit(solution)/shard_map/triangular_solve/custom-call.9 | solution.py:93
  1362.0 7.1 fusion.14
  1383.0 7.8 pad_maximum_fusion
  (190 shorter events, 121.8 us)
Async XLA Ops:
  7.2 156.4 %all-gather.2.cloned.1.call-start = ((), (), s32[]{:S(2)}) async-start(), calls=%async_computation.1 | async-start | bytes 13107200 | tf_op jit(solution)/shard_map/all_gather | solution.py:59
  61.0 305.3 %reduce-scatter.2.cloned.1.call-start = ((), (), s32[]{:S(2)}) async-start(), calls=%async_computation.2 | async-start | bytes 18874368 | tf_op jit(solution)/shard_map/reduce_scatter | solution.py:64
  175.8 190.5 %copy-start.18 = (f32[256]{0:T(256)S(1)}, f32[256]{0:T(256)}, u32[]{:S(2)}) copy-start(f32[256]{0:T(256)} %param.12) | copy-start | bytes 3076
  175.8 291.1 %all-reduce.12.cloned.1.call-start = ((), (), s32[]{:S(2)}) async-start(), calls=%async_computation.3 | async-start | bytes 8388608 | tf_op jit(solution)/shard_map/psum | solution.py:84
  368.0 98.9 %copy-start = (f32[256,2048]{0,1:T(8,128)}, f32[256,2048]{0,1:T(8,128)S(1)}, u32[]{:S(2)}) copy-start(f32[256,2048]{0,1:T(8,128)S(1)} %select_add_fusion) | copy-start | bytes 6291460
  371.2 282.4 %all-reduce.14.cloned.1.call-start = ((), (), s32[]{:S(2)}) async-start(), calls=%async_computation.4 | async-start | bytes 8388608 | tf_op jit(solution)/shard_map/psum | solution.py:84
  466.9 238.4 %all-reduce.22.cloned.1.call-start = ((), (), s32[]{:S(2)}) async-start(), calls=%async_computation.8 | async-start | bytes 3145728 | tf_op jit(solution)/shard_map/psum | solution.py:13
  655.9 315.9 %all-reduce.16.cloned.1.call-start = ((), (), s32[]{:S(2)}) async-start(), calls=%async_computation.5 | async-start | bytes 8388608 | tf_op jit(solution)/shard_map/psum | solution.py:84
  800.8 48.4 %copy-start.3 = (f32[512,512]{1,0:T(8,128)}, f32[512,512]{1,0:T(8,128)S(1)}, u32[]{:S(2)}) copy-start(f32[512,512]{1,0:T(8,128)S(1)} %get-tuple-element.208) | copy-start | bytes 3145732
  856.4 8.3 copy-start.16
  856.4 13.2 copy-start.1
  856.4 13.2 copy-start.4
  856.4 13.2 copy-start.6
  856.4 13.2 copy-start.8
  864.6 8.9 copy-start.10
  873.5 1.3 copy-start.14
  878.0 280.9 %all-reduce.18.cloned.1.call-start = ((), (), s32[]{:S(2)}) async-start(), calls=%async_computation.6 | async-start | bytes 8388608 | tf_op jit(solution)/shard_map/psum | solution.py:84
  971.9 189.4 %copy-start.5 = (f32[128,2048]{0,1:T(8,128)S(1)}, f32[128,2048]{0,1:T(8,128)}, u32[]{:S(2)}) copy-start(f32[128,2048]{0,1:T(8,128)} %copy.69) | copy-start | bytes 3145732
  971.9 189.4 %copy-start.7 = (f32[128,2048]{0,1:T(8,128)S(1)}, f32[128,2048]{0,1:T(8,128)}, u32[]{:S(2)}) copy-start(f32[128,2048]{0,1:T(8,128)} %copy.70) | copy-start | bytes 3145732
  971.9 189.4 %copy-start.9 = (f32[128,2048]{0,1:T(8,128)S(1)}, f32[128,2048]{0,1:T(8,128)}, u32[]{:S(2)}) copy-start(f32[128,2048]{0,1:T(8,128)} %copy.71) | copy-start | bytes 3145732
  971.9 239.1 %all-reduce.20.cloned.1.call-start = ((), (), s32[]{:S(2)}) async-start(), calls=%async_computation.7 | async-start | bytes 3145728 | tf_op jit(solution)/shard_map/psum | solution.py:13
  1306.3 48.4 %copy-start.2 = (f32[512,512]{1,0:T(8,128)}, f32[512,512]{1,0:T(8,128)S(1)}, u32[]{:S(2)}) copy-start(f32[512,512]{1,0:T(8,128)S(1)} %get-tuple-element.207) | copy-start | bytes 3145732
  1362.0 8.1 copy-start.17
  1362.0 13.0 copy-start.11
  1362.0 13.0 copy-start.12
  1362.0 13.0 copy-start.13
  1375.0 2.5 copy-start.15
Sparse Core Ops, SparseCore 0:
  61.1 102.4 all-gather.1
  175.9 190.3 reduce-scatter.1
  371.4 95.4 all-reduce.11
  469.3 184.2 all-reduce.13
  656.6 48.6 all-reduce.21
  878.2 93.6 all-reduce.15
  974.5 184.3 all-reduce.17
  1162.3 48.6 all-reduce.19
